TPU v7x, 32 devices: a whole 2x2x4 slice. The times are simulated.
32 devices in a mesh: dp: 2 (over x), seq: 8 (over z, core), tensor: 2 (over y).
Axes of the slice: x: 2, y: 2, z: 4, core: 2. Of those that a mesh axis runs over, the one named last changes fastest.
Arguments:
- queries: bfloat16 [2, 2048, 2048], P('dp', 'seq', 'tensor'), may hold values from -100 to 100
- image_keys: bfloat16 [2, 256, 256], P('dp', 'seq', 'tensor'), may hold values from -9 to 9
- image_states: bfloat16 [2, 256, 8192], P('dp', 'seq'), may hold values from -6 to 6
- value_weight: bfloat16 [8192, 256], P('seq', 'tensor'), may hold values from -0.0625 to 0.0625
- out_grad: bfloat16 [2, 2048, 2048], P('dp', 'seq', 'tensor'), may hold values from -6 to 6
Outputs:
- query_grad: bfloat16 [2, 2048, 2048], P('dp', 'seq', 'tensor')
- key_grad: bfloat16 [2, 256, 256], P('dp', 'seq', 'tensor')
- weight_grad: bfloat16 [8192, 256], P('seq', 'tensor')
- image_grad: bfloat16 [2, 256, 8192], P('dp', 'seq', 'tensor')
All inputs are finite; a program needn't handle non-finite values.
Results may differ from a plain program's by a relative error of at most 0.02.
Values may be sent and summed in bfloat16 or wider, within the bound.
A program may use at most 64 MiB of HBM per device.

v0:
```python
import math

import jax
import jax.numpy as jnp
from jax import lax
from jax.sharding import PartitionSpec as P

HD = 128


def attend(query_block, grad_block, keys_all, values_all):
    inv_root = 1.0 / math.sqrt(HD)
    image_total = keys_all.shape[0]
    text_rows, kv_local, heads_per = (
        query_block.shape[0],
        query_block.shape[1],
        query_block.shape[2],
    )
    text_span = math.gcd(text_rows, 128)
    block_count = text_rows // text_span
    key_rows = keys_all.reshape(image_total, kv_local, HD)
    value_rows = values_all.reshape(image_total, kv_local, HD)
    query_blocks = query_block.reshape(block_count, text_span, kv_local, heads_per, HD)
    grad_blocks = grad_block.reshape(block_count, text_span, kv_local, heads_per, HD)

    def text_step(running, blocks):
        key_acc, value_acc = running
        query_part, grad_part = blocks
        raw = (
            jnp.einsum("tkgd,jkd->tkgj", query_part, key_rows, preferred_element_type=jnp.float32)
            * inv_root
        )
        slopes = jnp.einsum(
            "tkgd,jkd->tkgj", grad_part, value_rows, preferred_element_type=jnp.float32
        )
        highest = raw.max(-1, keepdims=True)
        expo = jnp.exp(raw - highest)
        probs = expo / expo.sum(-1, keepdims=True)
        row_delta = (probs * slopes).sum(-1, keepdims=True)
        dscores = (probs * (slopes - row_delta) * inv_root).astype(jnp.bfloat16)
        probs_low = probs.astype(jnp.bfloat16)
        query_out = jnp.einsum(
            "tkgj,jkd->tkgd", dscores, key_rows, preferred_element_type=jnp.float32
        ).astype(jnp.bfloat16)
        key_acc = key_acc + jnp.einsum(
            "tkgj,tkgd->jkd", dscores, query_part, preferred_element_type=jnp.float32
        )
        value_acc = value_acc + jnp.einsum(
            "tkgj,tkgd->jkd", probs_low, grad_part, preferred_element_type=jnp.float32
        )
        return ((key_acc, value_acc), query_out)

    zero_grad = jnp.zeros((image_total, kv_local, HD), jnp.float32)
    (key_acc, value_acc), query_outs = lax.scan(
        text_step, (zero_grad, zero_grad), (query_blocks, grad_blocks)
    )
    return (
        query_outs,
        key_acc.reshape(image_total, kv_local * HD),
        value_acc.reshape(image_total, kv_local * HD),
    )


def on_device(queries, image_keys, image_states, value_weight, out_grad):
    kv_columns = image_keys.shape[2]
    kv_local = kv_columns // HD
    text_rows = queries.shape[1]
    heads_per = queries.shape[2] // kv_columns
    states = image_states[0]
    weight_full = lax.all_gather(value_weight, "seq", axis=0, tiled=True)
    values_own = jnp.dot(states, weight_full, preferred_element_type=jnp.float32).astype(
        jnp.bfloat16
    )
    keys_all, values_all = (
        lax.all_gather(image_keys[0], "seq", axis=0, tiled=True),
        lax.all_gather(values_own, "seq", axis=0, tiled=True),
    )
    query_block = queries[0].reshape(text_rows, kv_local, heads_per, HD)
    grad_block = out_grad[0].reshape(text_rows, kv_local, heads_per, HD)
    query_outs, key_partial, value_partial = attend(query_block, grad_block, keys_all, values_all)
    query_grad = query_outs.reshape(1, text_rows, heads_per * kv_columns)
    key_own, value_own = (
        lax.psum_scatter(
            key_partial.astype(jnp.bfloat16), "seq", scatter_dimension=0, tiled=True
        ).astype(jnp.float32),
        lax.psum_scatter(
            value_partial.astype(jnp.bfloat16), "seq", scatter_dimension=0, tiled=True
        ).astype(jnp.float32),
    )
    value_low = value_own.astype(jnp.bfloat16)
    weight_local = lax.psum_scatter(
        lax.dot_general(
            states, value_low, (((0,), (0,)), ((), ())), preferred_element_type=jnp.float32
        ).astype(jnp.bfloat16),
        "seq",
        scatter_dimension=0,
        tiled=True,
    )
    image_term = lax.dot_general(
        value_low, weight_full, (((1,), (1,)), ((), ())), preferred_element_type=jnp.float32
    )
    weight_grad = lax.psum(weight_local, "dp")
    image_grad = lax.psum_scatter(
        image_term.astype(jnp.bfloat16), "tensor", scatter_dimension=1, tiled=True
    )[None]
    return (query_grad, key_own.astype(jnp.bfloat16)[None], weight_grad, image_grad)


def solution(mesh):
    in_specs = (
        P("dp", "seq", "tensor"),
        P("dp", "seq", "tensor"),
        P("dp", "seq", None),
        P("seq", "tensor"),
        P("dp", "seq", "tensor"),
    )
    out_specs = (
        P("dp", "seq", "tensor"),
        P("dp", "seq", "tensor"),
        P("seq", "tensor"),
        P("dp", "seq", "tensor"),
    )
    return jax.shard_map(
        on_device, mesh=mesh, in_specs=in_specs, out_specs=out_specs, check_vma=False
    )
```

profile of v0, /device:TPU:0, one launch (start us, length us, event | category | flops | bytes accessed | tf_op | source)
XLA Modules:
  0.0 211.2 jit_solution(18442510026399107984)
XLA Ops:
  7.2 0.0 copy-start
  7.2 0.0 copy-start.3
  7.2 0.0 all-gather.3.cloned.1.call-start
  7.2 0.7 all-gather.3.cloned.1.call-update
  7.9 0.0 reduce-scatter.13.cloned.1.call-start
  8.0 1.1 copy.36
  9.1 1.1 copy.37
  10.3 15.7 %all-gather = bf16[1,256,128]{2,1,0:T(8,128)(2,1)S(1)} all-gather(bf16[1,32,128]{2,1,0:T(8,128)(2,1)S(1)} %copy-done.3), channel_id=2, replica_groups=mesh['dp'=2,'seq'=8,'tensor'=2] {'seq'}, dimensions={1}, use_global_device_ids=true | all-gather | bytes 73728 | tf_op jit(solution)/shard_map/all_gather | solution.py:75
  26.0 15.6 %all-gather.3.cloned.1.call-done = bf16[8192,128]{1,0:T(8,128)(2,1)} async-done(((bf16[1024,128]{1,0:T(8,128)(2,1)}), bf16[8192,128]{1,0:T(8,128)(2,1)}) %all-gather.3.cloned.1.call-update) | async-done | bytes 2097168 | tf_op jit(solution)/shard_map/all_gather | solution.py:70
  41.5 2.0 convolution_convert_fusion.3
  43.6 14.0 %all_gather.11 = bf16[256,128]{1,0:T(8,128)(2,1)S(1)} all-gather(bf16[32,128]{1,0:T(8,128)(2,1)S(1)} %convolution_convert_fusion.3), channel_id=1, replica_groups=mesh['dp'=2,'seq'=8,'tensor'=2] {'seq'}, dimensions={0}, use_global_device_ids=true | all-gather | bytes 73728 | tf_op jit(solution)/shard_map/all_gather | solution.py:76
  57.6 7.0 %while.15 = (s32[]{:T(128)}, f32[256,1,128]{0,2,1:T(8,128)S(1)}, f32[256,1,128]{0,2,1:T(8,128)S(1)}, bf16[2,128,1,8,128]{4,3,1,0,2:T(8,128)(2,1)S(1)}, bf16[2,12...) while((s32[]{:T(128)}, f32[256,1,128]{0,2,1:T(8,128)S(1)}, ...), condition=%wide.region_4.5_spmd.clone, body=%wide.region_0.4_spmd.clone.sunk | while | flops 340259840 | bytes 12562560 | solution.py:54
  57.6 0.4 fusion.37
  58.0 0.4 fusion.38
  58.4 0.6 fusion.41
  59.0 0.7 multiply_reduce_fusion.2
  59.7 0.5 fusion.39
  60.2 0.3 fusion.40
  60.5 0.3 fusion.42
  60.8 0.2 copy_dynamic-update-slice_fusion.2
  61.1 0.4 fusion.37
  61.5 0.4 fusion.38
  61.9 0.6 fusion.41
  62.5 0.7 multiply_reduce_fusion.2
  63.2 0.5 fusion.39
  63.7 0.3 fusion.40
  64.0 0.3 fusion.42
  64.3 0.2 copy_dynamic-update-slice_fusion.2
  64.6 0.7 copy.30
  65.3 0.0 reduce-scatter.13.cloned.1.call-update
  65.3 0.0 reduce-scatter.9.cloned.1.call-start
  65.4 29.7 %reduce-scatter.13.cloned.1.call-done = bf16[32,128]{1,0:T(8,128)(2,1)} async-done(((bf16[256,128]{1,0:T(8,128)(2,1)}), bf16[32,128]{1,0:T(8,128)(2,1)}) %reduce-scatter.13.cloned.1.call-update) | async-done | bytes 8208
  95.0 2.8 %fusion.13 = bf16[8192,128]{0,1:T(8,128)(2,1)} fusion(bf16[32,128]{1,0:T(8,128)(2,1)} %reduce-scatter.13.cloned.1.call-done, bf16[1,32,8192]{2,1,0:T(8,128)(2,1)S(1)} %copy-done), kind=kOutput, calls=%fused_computation.26 | convolution fusion | flops 68157440 | bytes 2629632 | tf_op jit(solution)/shard_map/dot_general | solution.py:92
  97.9 0.0 reduce-scatter.9.cloned.1.call-update
  97.9 0.0 all-reduce.2.cloned.1.call-start
  97.9 34.0 %reduce-scatter.9.cloned.1.call-done = bf16[1024,128]{0,1:T(8,128)(2,1)} async-done(((bf16[8192,128]{0,1:T(8,128)(2,1)}), bf16[1024,128]{0,1:T(8,128)(2,1)}) %reduce-scatter.9.cloned.1.call-update) | async-done | bytes 262160 | tf_op jit(solution)/shard_map/reduce_scatter | solution.py:91
  131.9 0.0 all-reduce.2.cloned.1.call-update
  132.0 0.0 reduce-scatter.7.cloned.1.call-start
  132.0 0.7 copy.26
  132.7 0.0 reduce-scatter.7.cloned.1.call-update
  132.8 0.0 reduce-scatter.11.cloned.1.call-start
  132.8 1.6 convolution_convert_fusion.2
  134.5 0.0 reduce-scatter.11.cloned.1.call-update
  134.5 1.0 reshape.72
  135.5 20.6 %all-reduce.2.cloned.1.call-done = bf16[1024,128]{0,1:T(8,128)(2,1)} async-done(((bf16[1024,128]{0,1:T(8,128)(2,1)}), bf16[1024,128]{0,1:T(8,128)(2,1)}) %all-reduce.2.cloned.1.call-update) | async-done | bytes 262160 | tf_op jit(solution)/shard_map/psum | solution.py:102
  156.1 1.8 copy.27
  157.9 30.9 %reduce-scatter.7.cloned.1.call-done = bf16[32,128]{1,0:T(8,128)(2,1)} async-done(((bf16[256,128]{1,0:T(8,128)(2,1)}), bf16[32,128]{1,0:T(8,128)(2,1)}) %reduce-scatter.7.cloned.1.call-update) | async-done | bytes 8208 | tf_op jit(solution)/shard_map/reduce_scatter | solution.py:83
  188.8 15.5 %reduce-scatter.11.cloned.1.call-done = bf16[32,4096]{1,0:T(8,128)(2,1)} async-done(((bf16[32,8192]{1,0:T(8,128)(2,1)}), bf16[32,4096]{1,0:T(8,128)(2,1)}) %reduce-scatter.11.cloned.1.call-update) | async-done | bytes 262160 | tf_op jit(solution)/shard_map/reduce_scatter | solution.py:103
  (12 shorter events, 0.1 us)
Async XLA Ops:
  7.2 34.4 %copy-start = (bf16[1,32,8192]{2,1,0:T(8,128)(2,1)S(1)}, bf16[1,32,8192]{2,1,0:T(8,128)(2,1)}, u32[]{:S(2)}) copy-start(bf16[1,32,8192]{2,1,0:T(8,128)(2,1)} %param.9) | copy-start | bytes 1572868
  7.2 3.1 %copy-start.3 = (bf16[1,32,128]{2,1,0:T(8,128)(2,1)S(1)}, bf16[1,32,128]{2,1,0:T(8,128)(2,1)}, u32[]{:S(2)}) copy-start(bf16[1,32,128]{2,1,0:T(8,128)(2,1)} %param.8) | copy-start | bytes 24580
  7.2 34.4 %all-gather.3.cloned.1.call-start = ((), (), s32[]{:S(2)}) async-start(), calls=%async_computation.4 | async-start | bytes 2359296 | tf_op jit(solution)/shard_map/all_gather | solution.py:70
  7.9 87.1 %reduce-scatter.13.cloned.1.call-start = ((), (), s32[]{:S(2)}) async-start(), calls=%async_computation.9 | async-start | bytes 73728
  65.3 67.5 %copy-start.1 = (bf16[8192,128]{1,0:T(8,128)(2,1)S(1)}, bf16[8192,128]{1,0:T(8,128)(2,1)}, u32[]{:S(2)}) copy-start(bf16[8192,128]{1,0:T(8,128)(2,1)} %all-gather.3.cloned.1.call-done) | copy-start | bytes 6291460
  65.3 66.6 %reduce-scatter.9.cloned.1.call-start = ((), (), s32[]{:S(2)}) async-start(), calls=%async_computation.6 | async-start | bytes 2359296 | tf_op jit(solution)/shard_map/reduce_scatter | solution.py:91
  95.0 37.8 %copy-start.2 = (bf16[32,128]{1,0:T(8,128)(2,1)S(1)}, bf16[32,128]{1,0:T(8,128)(2,1)}, u32[]{:S(2)}) copy-start(bf16[32,128]{1,0:T(8,128)(2,1)} %reduce-scatter.13.cloned.1.call-done) | copy-start | bytes 24580
  97.9 58.3 %all-reduce.2.cloned.1.call-start = ((), (), s32[]{:S(2)}) async-start(), calls=%async_computation.7 | async-start | bytes 524288 | tf_op jit(solution)/shard_map/psum | solution.py:102
  132.0 56.9 %reduce-scatter.7.cloned.1.call-start = ((), (), s32[]{:S(2)}) async-start(), calls=%async_computation.5 | async-start | bytes 73728 | tf_op jit(solution)/shard_map/reduce_scatter | solution.py:83
  132.8 71.6 %reduce-scatter.11.cloned.1.call-start = ((), (), s32[]{:S(2)}) async-start(), calls=%async_computation.8 | async-start | bytes 786432 | tf_op jit(solution)/shard_map/reduce_scatter | solution.py:103
Sparse Core Ops, SparseCore 0:
  9.6 31.8 all-gather.2
  65.4 29.5 reduce-scatter.12
  98.0 33.9 reduce-scatter.8
  134.2 21.9 all-reduce.1
  158.8 30.0 reduce-scatter.6
  191.6 12.6 reduce-scatter.10
where the time goes:
time: 211 us
  waiting for transfers between devices  147 us (70%)
  blocking collectives  29.6 us (14%)
  between operations  14.2 us (7%)
  matrix products  11.1 us (5%)
  local copies, waits for them, and re-layouts  7.03 us (3%)
    reduce_scatter x1, waiting for transfers between devices, on_device(): lax.psum_scatter(lax.dot_general(states, value_low, (((0,), (0,)), ((), (...  34 us
    reduce_scatter x1, waiting for transfers between devices, on_device(): lax.psum_scatter(key_partial.astype(jnp.bfloat16), 'seq', scatter_dimensi...  30.9 us
    unnamed x7, waiting for transfers between devices  30.4 us
    psum x1, waiting for transfers between devices, on_device(): weight_grad = lax.psum(weight_local, 'dp')  20.6 us
    all_gather x1, blocking collectives, on_device(): lax.all_gather(image_keys[0], 'seq', axis=0, tiled=True)  15.7 us
    all_gather x1, waiting for transfers between devices, on_device(): weight_full = lax.all_gather(value_weight, 'seq', axis=0, tiled=True)  15.6 us
    reduce_scatter x1, waiting for transfers between devices, on_device(): lax.psum_scatter(image_term.astype(jnp.bfloat16), 'tensor', scatter_dimen...  15.5 us
    all_gather x1, blocking collectives, on_device(): lax.all_gather(values_own, 'seq', axis=0, tiled=True)  14 us
  transfers between devices with their start and end apart: 6, of which 6 were waited for; matrix products, arithmetic and copies ran while one was open for 4% of the time, Pallas kernels for 0%

commit v1 on v0

v1 whole, which is shorter than its diff:
```python
import functools
import math

import jax
import jax.numpy as jnp
from jax import lax
from jax.experimental import pallas as pl
from jax.experimental.pallas import tpu as pltpu
from jax.sharding import PartitionSpec as P

HD = 128
MESH = pl.DeviceIdType.MESH
F32 = jnp.float32
BF16 = jnp.bfloat16


def dot(a, b, a_dim, b_dim):
    return lax.dot_general(a, b, (((a_dim,), (b_dim,)), ((), ())), preferred_element_type=F32)


def kernel(
    n_dp, n_seq, n_t,
    q_ref, k_ref, st_ref, w_ref, og_ref,
    qg_ref, kg_ref, wg_ref, ig_ref,
    keys_all, scol, w_all, probs, vp_acc, vp_send, vp_recv, xp_send, xp_recv,
    vg_all, val_all, kp_acc, kp_send, kp_recv, wg_send, wg_recv, ig_send, ig_recv,
    keys_ss, keys_rs, st_ss, st_rs, w_ss, w_rs, vp_ss, vp_rs, xp_ss, xp_rs,
    vg_ss, vg_rs, val_ss, val_rs, kp_ss, kp_rs, wg_ss, wg_rs, ig_ss, ig_rs,
):
    d, s, t = lax.axis_index("dp"), lax.axis_index("seq"), lax.axis_index("tensor")
    img_dev = k_ref.shape[1]
    image_total = n_seq * img_dev
    text_rows = q_ref.shape[1]
    heads = q_ref.shape[2] // HD
    d_seq = w_ref.shape[0]
    per_t = n_seq // n_t
    inv_root = 1.0 / math.sqrt(HD)

    def plus(a, b, n):
        return lax.rem(a + b, n)

    def minus(a, b, n):
        return lax.rem(a - b + n, n)

    def remote(src, dst, send, recv, device):
        return pltpu.make_async_remote_copy(
            src_ref=src, dst_ref=dst, send_sem=send, recv_sem=recv,
            device_id=device, device_id_type=MESH,
        )

    def over_seq(fn):
        pl.loop(1, n_seq)(fn)

    barrier = pltpu.get_barrier_semaphore()

    @pl.loop(1, n_seq * n_t)
    def _(m):
        pl.semaphore_signal(
            barrier, inc=1,
            device_id={"seq": plus(s, m // n_t, n_seq), "tensor": plus(t, m % n_t, n_t)},
            device_id_type=MESH,
        )

    for kd in range(1, n_dp):
        pl.semaphore_signal(
            barrier, inc=1, device_id={"dp": plus(d, kd, n_dp)}, device_id_type=MESH
        )
    pl.semaphore_wait(barrier, n_seq * n_t - 1 + n_dp - 1)

    def keys_copy(k):
        return remote(k_ref.at[0], keys_all.at[s], keys_ss.at[k], keys_rs.at[k],
                      {"seq": plus(s, k, n_seq)})

    @over_seq
    def _(k):
        keys_copy(k).start()

    def st_copy(k):
        to = plus(s, k, n_seq)
        cols = pl.ds(pl.multiple_of(to * d_seq, d_seq), d_seq)
        return remote(st_ref.at[0, :, cols], scol.at[s], st_ss.at[k], st_rs.at[k], {"seq": to})

    @over_seq
    def _(k):
        st_copy(k).start()

    def w_copy(k):
        return remote(w_ref, w_all.at[t], w_ss.at[k], w_rs.at[k], {"tensor": plus(t, k, n_t)})

    for k in range(1, n_t):
        w_copy(k).start()

    keys_all[s] = k_ref[0]
    scol[s] = st_ref[0, :, pl.ds(pl.multiple_of(s * d_seq, d_seq), d_seq)]
    w_all[t] = w_ref[...]

    def landed(buffer, send, recv, k):
        source = buffer.at[minus(s, k, n_seq)]
        return remote(source, source, send.at[k], recv.at[k], {"seq": plus(s, k, n_seq)})

    @over_seq
    def _(k):
        landed(keys_all, keys_ss, keys_rs, k).wait_recv()

    vp_acc[...] = jnp.zeros_like(vp_acc)

    @pl.loop(0, heads)
    def _(h):
        cols = pl.ds(pl.multiple_of(h * HD, HD), HD)
        keys = keys_all[...].reshape(image_total, HD)
        raw = dot(keys, q_ref[0, :, cols], 1, 1) * inv_root
        expo = jnp.exp(raw - raw.max(0, keepdims=True))
        p = expo * (1.0 / expo.sum(0, keepdims=True))
        probs[h] = p
        vp_acc[...] += dot(p.astype(BF16), og_ref[0, :, cols], 1, 0)

    vp_send[...] = vp_acc[...].astype(BF16).reshape(n_seq, img_dev, HD)

    def scatter_copy(src, dst, send, recv, k):
        to = plus(s, k, n_seq)
        return remote(src.at[to], dst.at[s], send.at[k], recv.at[k], {"seq": to})

    @over_seq
    def _(k):
        scatter_copy(vp_send, vp_recv, vp_ss, vp_rs, k).start()

    vp_recv[s] = vp_send[s]

    @over_seq
    def _(k):
        landed(vp_recv, vp_ss, vp_rs, k).wait_recv()

    vg_all[t, s] = vp_recv[...].astype(F32).sum(0).astype(BF16)

    def vg_copy(m):
        return remote(
            vg_all.at[t, s], vg_all.at[t, s], vg_ss.at[m], vg_rs.at[m],
            {"seq": plus(s, m // n_t, n_seq), "tensor": plus(t, m % n_t, n_t)},
        )

    @pl.loop(1, n_seq * n_t)
    def _(m):
        vg_copy(m).start()

    @over_seq
    def _(k):
        landed(scol, st_ss, st_rs, k).wait_recv()

    states = scol[...].reshape(image_total, d_seq)
    xp_send[...] = dot(states, w_ref[...], 1, 0).reshape(n_seq, img_dev, HD)

    @over_seq
    def _(k):
        scatter_copy(xp_send, xp_recv, xp_ss, xp_rs, k).start()

    xp_recv[s] = xp_send[s]

    @pl.loop(1, n_seq * n_t)
    def _(m):
        source = vg_all.at[minus(t, m % n_t, n_t), minus(s, m // n_t, n_seq)]
        remote(source, source, vg_ss.at[m], vg_rs.at[m],
               {"seq": plus(s, m // n_t, n_seq), "tensor": plus(t, m % n_t, n_t)}).wait_recv()

    vg_own = vg_all[t].reshape(image_total, HD)
    wg_send[...] = dot(scol[...].reshape(image_total, d_seq), vg_own, 0, 0).astype(BF16)

    def wg_copy(k):
        return remote(wg_send, wg_recv.at[d], wg_ss.at[k], wg_rs.at[k], {"dp": plus(d, k, n_dp)})

    for k in range(1, n_dp):
        wg_copy(k).start()

    for k in range(1, n_t):
        source = w_all.at[minus(t, k, n_t)]
        remote(source, source, w_ss.at[k], w_rs.at[k], {"tensor": plus(t, k, n_t)}).wait_recv()

    def image_term(c):
        rows = jnp.concatenate([vg_all[c, j * n_t + t] for j in range(per_t)], axis=0)
        return dot(rows, w_all[c], 1, 1).astype(BF16).astype(F32)

    total = image_term(0)
    for c in range(1, n_t):
        total = total + image_term(c)
    ig_send[...] = total.astype(BF16).reshape(per_t, img_dev, d_seq)

    to_t = s // per_t
    slot = pl.ds(pl.multiple_of(lax.rem(s, per_t) * d_seq, d_seq), d_seq)

    def ig_copy(j):
        return remote(ig_send.at[j], ig_recv.at[:, slot], ig_ss.at[j], ig_rs.at[lax.rem(s, per_t)],
                      {"seq": j * n_t + t, "tensor": to_t})

    def ig_stays(j):
        return jnp.logical_and(j * n_t + t == s, to_t == t)

    for j in range(per_t):
        @pl.when(jnp.logical_not(ig_stays(j)))
        def _():
            ig_copy(j).start()

        @pl.when(ig_stays(j))
        def _():
            ig_recv[:, slot] = ig_send[j]

    @over_seq
    def _(k):
        landed(xp_recv, xp_ss, xp_rs, k).wait_recv()

    val_all[s] = xp_recv[...].sum(0).astype(BF16)

    def val_copy(k):
        return remote(val_all.at[s], val_all.at[s], val_ss.at[k], val_rs.at[k],
                      {"seq": plus(s, k, n_seq)})

    @over_seq
    def _(k):
        val_copy(k).start()

    @over_seq
    def _(k):
        landed(val_all, val_ss, val_rs, k).wait_recv()

    kp_acc[...] = jnp.zeros_like(kp_acc)

    @pl.loop(0, heads)
    def _(h):
        cols = pl.ds(pl.multiple_of(h * HD, HD), HD)
        slopes = dot(val_all[...].reshape(image_total, HD), og_ref[0, :, cols], 1, 1)
        p = probs[h]
        delta = (p * slopes).sum(0, keepdims=True)
        ds = (p * (slopes - delta) * inv_root).astype(BF16)
        kp_acc[...] += dot(ds, q_ref[0, :, cols], 1, 0)
        keys = keys_all[...].reshape(image_total, HD)
        qg_ref[0, :, cols] = dot(ds, keys, 0, 0).astype(BF16)

    kp_send[...] = kp_acc[...].astype(BF16).reshape(n_seq, img_dev, HD)

    @over_seq
    def _(k):
        scatter_copy(kp_send, kp_recv, kp_ss, kp_rs, k).start()

    kp_recv[s] = kp_send[s]

    wg_total = wg_send[...].astype(F32)
    for k in range(1, n_dp):
        source = wg_recv.at[minus(d, k, n_dp)]
        remote(source, source, wg_ss.at[k], wg_rs.at[k], {"dp": plus(d, k, n_dp)}).wait_recv()
        wg_total = wg_total + wg_recv[minus(d, k, n_dp)].astype(F32)
    wg_ref[...] = wg_total.astype(BF16)

    for j in range(per_t):
        from_s = t * per_t + j
        from_t = lax.rem(s, n_t)

        @pl.when(jnp.logical_not(jnp.logical_and(from_s == s, from_t == t)))
        def _():
            place = ig_recv.at[:, pl.ds(j * d_seq, d_seq)]
            remote(ig_send.at[0], place, ig_ss.at[j], ig_rs.at[j],
                   {"seq": from_s, "tensor": from_t}).wait_recv()

    ig_ref[0] = ig_recv[...]

    @over_seq
    def _(k):
        landed(kp_recv, kp_ss, kp_rs, k).wait_recv()

    kg_ref[0] = kp_recv[...].astype(F32).sum(0).astype(BF16)

    @over_seq
    def _(k):
        keys_copy(k).wait_send()
        st_copy(k).wait_send()
        scatter_copy(vp_send, vp_recv, vp_ss, vp_rs, k).wait_send()
        scatter_copy(xp_send, xp_recv, xp_ss, xp_rs, k).wait_send()
        val_copy(k).wait_send()
        scatter_copy(kp_send, kp_recv, kp_ss, kp_rs, k).wait_send()

    @pl.loop(1, n_seq * n_t)
    def _(m):
        vg_copy(m).wait_send()

    for k in range(1, n_t):
        w_copy(k).wait_send()
    for k in range(1, n_dp):
        wg_copy(k).wait_send()
    for j in range(per_t):
        @pl.when(jnp.logical_not(ig_stays(j)))
        def _():
            ig_copy(j).wait_send()


def on_device(n_dp, n_seq, n_t, queries, image_keys, image_states, value_weight, out_grad):
    img_dev = image_keys.shape[1]
    image_total = n_seq * img_dev
    text_rows = queries.shape[1]
    heads = queries.shape[2] // HD
    d_model = image_states.shape[2]
    d_seq = value_weight.shape[0]
    d_t = d_model // n_t
    per_t = n_seq // n_t
    vmem = pltpu.VMEM
    rows = (n_seq, img_dev, HD)
    scratch = [
        vmem(rows, BF16),
        vmem((n_seq, img_dev, d_seq), BF16),
        vmem((n_t, d_seq, HD), BF16),
        vmem((heads, image_total, text_rows), F32),
        vmem((image_total, HD), F32),
        vmem(rows, BF16),
        vmem(rows, BF16),
        vmem(rows, F32),
        vmem(rows, F32),
        vmem((n_t,) + rows, BF16),
        vmem(rows, BF16),
        vmem((image_total, HD), F32),
        vmem(rows, BF16),
        vmem(rows, BF16),
        vmem((d_seq, HD), BF16),
        vmem((n_dp, d_seq, HD), BF16),
        vmem((per_t, img_dev, d_seq), BF16),
        vmem((img_dev, d_t), BF16),
    ]
    counts = [n_seq, n_seq, n_t, n_seq, n_seq, n_seq * n_t, n_seq, n_seq, n_dp, per_t]
    sems = [pltpu.SemaphoreType.DMA((c,)) for c in counts for _ in range(2)]
    spec = pl.BlockSpec(memory_space=pltpu.VMEM)
    return pl.pallas_call(
        functools.partial(kernel, n_dp, n_seq, n_t),
        out_shape=(
            jax.ShapeDtypeStruct(queries.shape, BF16),
            jax.ShapeDtypeStruct(image_keys.shape, BF16),
            jax.ShapeDtypeStruct(value_weight.shape, BF16),
            jax.ShapeDtypeStruct((1, img_dev, d_t), BF16),
        ),
        in_specs=[spec] * 5,
        out_specs=(spec,) * 4,
        scratch_shapes=scratch + sems,
        compiler_params=pltpu.CompilerParams(
            collective_id=0, has_side_effects=True, vmem_limit_bytes=48 * 1024 * 1024
        ),
    )(queries, image_keys, image_states, value_weight, out_grad)


def solution(mesh):
    in_specs = (
        P("dp", "seq", "tensor"),
        P("dp", "seq", "tensor"),
        P("dp", "seq", None),
        P("seq", "tensor"),
        P("dp", "seq", "tensor"),
    )
    out_specs = (
        P("dp", "seq", "tensor"),
        P("dp", "seq", "tensor"),
        P("seq", "tensor"),
        P("dp", "seq", "tensor"),
    )
    sizes = (mesh.shape["dp"], mesh.shape["seq"], mesh.shape["tensor"])
    return jax.shard_map(
        functools.partial(on_device, *sizes),
        mesh=mesh, in_specs=in_specs, out_specs=out_specs, check_vma=False,
    )
```

time: 211 us -> 55.4 us (0.26)
  waiting for transfers between devices: 147 us -> 0 us
  Pallas kernels: 0 us -> 46.9 us
  blocking collectives: 29.6 us -> 0 us
  between operations: 14.2 us -> 0.65 us
  matrix products: 11.1 us -> 0 us
    reduce_scatter x3 -> x0, waiting for transfers between devices: 80.4 us -> none  [the longest x1 34 us: on_device(): lax.psum_scatter(lax.dot_general(states, value_low, (((0,), (0,)), ((), (...]
    pallas_call x0 -> x1, Pallas kernels: none -> 46.9 us  [on_device(): pl.pallas_call(functools.partial(kernel, n_dp, n_seq, n_t), out_shape=(ja...]
    unnamed x7 -> x0, waiting for transfers between devices: 30.4 us -> none
    all_gather x2 -> x0, blocking collectives: 29.6 us -> none  [the longest x1 15.7 us: on_device(): lax.all_gather(image_keys[0], 'seq', axis=0, tiled=True)]
    psum x1 -> x0, waiting for transfers between devices: 20.6 us -> none  [on_device(): weight_grad = lax.psum(weight_local, 'dp')]
    all_gather x1 -> x0, waiting for transfers between devices: 15.6 us -> none  [on_device(): weight_full = lax.all_gather(value_weight, 'seq', axis=0, tiled=True)]
    dot_general x13 -> x0, matrix products: 11.1 us -> none  [the longest x1 2.81 us: on_device(): lax.dot_general(states, value_low, (((0,), (0,)), ((), ())), preferred_el...]
    unnamed x12 -> x14, local copies, waits for them, and re-layouts: 4.82 us -> 7.56 us
  transfers between devices with their start and end apart: 6 -> 0, of which waited for: 6 -> 0; matrix products, arithmetic and copies ran while one was open for 4% -> 0% of each run, Pallas kernels for 0% -> 0%
where the time goes in v1:
time: 55.4 us; the launch traced here: 55.1 us
  Pallas kernels  46.9 us (85%)
  local copies, waits for them, and re-layouts  7.56 us (14%)
  between operations  0.65 us (1%)
    pallas_call x1, Pallas kernels, on_device(): pl.pallas_call(functools.partial(kernel, n_dp, n_seq, n_t), out_shape=(ja...  46.9 us
    unnamed x14, local copies, waits for them, and re-layouts  7.56 us

profile of v1, /device:TPU:0, one launch (start us, length us, event | category | flops | bytes accessed | tf_op | source)
XLA Modules:
  0.0 55.1 jit_solution(3609977347759156412)
XLA Ops:
  0.6 0.0 copy-start
  0.6 1.0 %copy-done = bf16[1,256,1024]{2,1,0:T(8,128)(2,1)S(1)} copy-done((bf16[1,256,1024]{2,1,0:T(8,128)(2,1)S(1)}, bf16[1,256,1024]{2,1,0:T(8,128)(2,1)}, u32[]{:S(2)}) %copy-start) | copy-done | bytes 524312
  1.7 0.0 copy-start.1
  1.7 1.0 %copy-done.1 = bf16[1,32,8192]{2,1,0:T(8,128)(2,1)S(1)} copy-done((bf16[1,32,8192]{2,1,0:T(8,128)(2,1)S(1)}, bf16[1,32,8192]{2,1,0:T(8,128)(2,1)}, u32[]{:S(2)}) %copy-start.1) | copy-done | bytes 524312
  2.7 0.0 copy-start.2
  2.7 1.0 %copy-done.2 = bf16[1,256,1024]{2,1,0:T(8,128)(2,1)S(1)} copy-done((bf16[1,256,1024]{2,1,0:T(8,128)(2,1)S(1)}, bf16[1,256,1024]{2,1,0:T(8,128)(2,1)}, u32[]{:S(2)}) %copy-start.2) | copy-done | bytes 524312
  3.8 0.0 copy-start.3
  3.8 0.9 %copy-done.3 = bf16[1024,128]{1,0:T(8,128)(2,1)S(1)} copy-done((bf16[1024,128]{1,0:T(8,128)(2,1)S(1)}, bf16[1024,128]{1,0:T(8,128)(2,1)}, u32[]{:S(2)}) %copy-start.3) | copy-done | bytes 262168
  4.7 0.0 copy-start.4
  4.7 0.7 %copy-done.4 = bf16[1,32,128]{2,1,0:T(8,128)(2,1)S(1)} copy-done((bf16[1,32,128]{2,1,0:T(8,128)(2,1)S(1)}, bf16[1,32,128]{2,1,0:T(8,128)(2,1)}, u32[]{:S(2)}) %copy-start.4) | copy-done | bytes 8216
  5.4 46.9 %shard_map.84 = (bf16[1,256,1024]{2,1,0:T(8,128)(2,1)S(1)}, bf16[1,32,128]{2,1,0:T(8,128)(2,1)S(1)}, bf16[1024,128]{1,0:T(8,128)(2,1)S(1)}, bf16[1,32,4096]{2,1,0:T(8,128)(2,1)S(1)}) custom-call(bf16[1,256,1024]{2,1,0:T(8,128)(2,1)S(1)} %copy-done, bf16[1,32,128]{2,1,0:T(8,128)(2,1)S(1)} %copy-done.4, bf16[1,32,8192]{2,1,0:T(8,128)(2,1)S(1)} %copy-done.1, ...), custom_call_target="tpu_custom_call" | custom-call | tf_op jit(solution)/shard_map/pallas_call | solution.py:326
  52.3 0.8 %copy.13 = bf16[1,256,1024]{2,1,0:T(8,128)(2,1)} copy(bf16[1,256,1024]{2,1,0:T(8,128)(2,1)S(1)} %get-tuple-element.8) | data formatting | bytes 1048576
  53.1 0.6 %copy.14 = bf16[1,32,128]{2,1,0:T(8,128)(2,1)} copy(bf16[1,32,128]{2,1,0:T(8,128)(2,1)S(1)} %get-tuple-element.9) | data formatting | bytes 16384
  53.7 0.7 %copy.15 = bf16[1024,128]{1,0:T(8,128)(2,1)} copy(bf16[1024,128]{1,0:T(8,128)(2,1)S(1)} %get-tuple-element.10) | data formatting | bytes 524288
  54.4 0.7 %copy.16 = bf16[1,32,4096]{2,1,0:T(8,128)(2,1)} copy(bf16[1,32,4096]{2,1,0:T(8,128)(2,1)S(1)} %get-tuple-element.11) | data formatting | bytes 524288
Async XLA Ops:
  0.6 1.0 %copy-start = (bf16[1,256,1024]{2,1,0:T(8,128)(2,1)S(1)}, bf16[1,256,1024]{2,1,0:T(8,128)(2,1)}, u32[]{:S(2)}) copy-start(bf16[1,256,1024]{2,1,0:T(8,128)(2,1)} %q_ref.1) | copy-start | bytes 1572868
  1.7 1.0 %copy-start.1 = (bf16[1,32,8192]{2,1,0:T(8,128)(2,1)S(1)}, bf16[1,32,8192]{2,1,0:T(8,128)(2,1)}, u32[]{:S(2)}) copy-start(bf16[1,32,8192]{2,1,0:T(8,128)(2,1)} %st_ref.1) | copy-start | bytes 1572868
  2.7 1.0 %copy-start.2 = (bf16[1,256,1024]{2,1,0:T(8,128)(2,1)S(1)}, bf16[1,256,1024]{2,1,0:T(8,128)(2,1)}, u32[]{:S(2)}) copy-start(bf16[1,256,1024]{2,1,0:T(8,128)(2,1)} %og_ref.1) | copy-start | bytes 1572868
  3.8 0.9 %copy-start.3 = (bf16[1024,128]{1,0:T(8,128)(2,1)S(1)}, bf16[1024,128]{1,0:T(8,128)(2,1)}, u32[]{:S(2)}) copy-start(bf16[1024,128]{1,0:T(8,128)(2,1)} %w_ref.1) | copy-start | bytes 786436
  4.7 0.7 %copy-start.4 = (bf16[1,32,128]{2,1,0:T(8,128)(2,1)S(1)}, bf16[1,32,128]{2,1,0:T(8,128)(2,1)}, u32[]{:S(2)}) copy-start(bf16[1,32,128]{2,1,0:T(8,128)(2,1)} %k_ref.1) | copy-start | bytes 24580

commit v2 on v1

v2 whole, which is shorter than its diff:
```python
import functools
import math

import jax
import jax.numpy as jnp
from jax import lax
from jax.experimental import pallas as pl
from jax.experimental.pallas import tpu as pltpu
from jax.sharding import PartitionSpec as P

HD = 128
MESH = pl.DeviceIdType.MESH
F32 = jnp.float32
BF16 = jnp.bfloat16
XP = jnp.bfloat16


def dot(a, b, a_dim, b_dim):
    return lax.dot_general(a, b, (((a_dim,), (b_dim,)), ((), ())), preferred_element_type=F32)


def kernel(
    n_dp, n_seq, n_t,
    q_hbm, k_hbm, st_hbm, w_hbm, og_hbm,
    qg_hbm, kg_hbm, wg_hbm, ig_hbm,
    qg_ref, kg_ref, wg_ref, ig_ref, q_ref, og_ref, keys_all, scol, w_all, probs, vp_acc, vp_send, vp_recv, xp_send, xp_recv,
    vg_all, val_all, kp_acc, kp_send, kp_recv, wg_send, wg_recv, ig_send, ig_recv,
    out_sem, in_sem, keys_ss, keys_rs, st_ss, st_rs, w_ss, w_rs, vp_ss, vp_rs, xp_ss, xp_rs,
    vg_ss, vg_rs, val_ss, val_rs, kp_ss, kp_rs, wg_ss, wg_rs, ig_ss, ig_rs,
):
    d, s, t = lax.axis_index("dp"), lax.axis_index("seq"), lax.axis_index("tensor")
    img_dev = k_hbm.shape[1]
    image_total = n_seq * img_dev
    text_rows = q_hbm.shape[1]
    heads = q_hbm.shape[2] // HD
    d_seq = w_hbm.shape[0]
    per_t = n_seq // n_t
    inv_root = 1.0 / math.sqrt(HD)

    def plus(a, b, n):
        return lax.rem(a + b, n)

    def minus(a, b, n):
        return lax.rem(a - b + n, n)

    def remote(src, dst, send, recv, device):
        return pltpu.make_async_remote_copy(
            src_ref=src, dst_ref=dst, send_sem=send, recv_sem=recv,
            device_id=device, device_id_type=MESH,
        )

    def over_seq(fn):
        pl.loop(1, n_seq)(fn)

    parts = n_t if d_seq % (n_t * 128) == 0 else 1
    width = d_seq // parts
    part = t % parts

    def cols_of(seq_index):
        return pl.ds(pl.multiple_of(seq_index * d_seq + part * width, width), width)

    def rows_of(c):
        return pl.ds(pl.multiple_of((c % parts) * width, width), width)

    locals_in = [
        pltpu.make_async_copy(k_hbm.at[0], keys_all.at[s], in_sem.at[0]),
        pltpu.make_async_copy(q_hbm, q_ref, in_sem.at[1]),
        pltpu.make_async_copy(og_hbm, og_ref, in_sem.at[2]),
        pltpu.make_async_copy(w_hbm, w_all.at[t], in_sem.at[3]),
        pltpu.make_async_copy(st_hbm.at[0, :, cols_of(s)], scol.at[s], in_sem.at[4]),
    ]

    barrier = pltpu.get_barrier_semaphore()

    @pl.loop(1, n_seq * n_t)
    def _(m):
        pl.semaphore_signal(
            barrier, inc=1,
            device_id={"seq": plus(s, m // n_t, n_seq), "tensor": plus(t, m % n_t, n_t)},
            device_id_type=MESH,
        )

    for kd in range(1, n_dp):
        for kt in range(parts):
            pl.semaphore_signal(
                barrier, inc=1,
                device_id={"dp": plus(d, kd, n_dp), "tensor": plus(t, kt, n_t)},
                device_id_type=MESH,
            )
    for copy in locals_in:
        copy.start()
    pl.semaphore_wait(barrier, n_seq * n_t - 1 + (n_dp - 1) * parts)

    def keys_copy(k):
        return remote(k_hbm.at[0], keys_all.at[s], keys_ss.at[k], keys_rs.at[k],
                      {"seq": plus(s, k, n_seq)})

    @over_seq
    def _(k):
        keys_copy(k).start()

    def st_copy(k):
        to = plus(s, k, n_seq)
        return remote(st_hbm.at[0, :, cols_of(to)], scol.at[s], st_ss.at[k], st_rs.at[k], {"seq": to})

    @over_seq
    def _(k):
        st_copy(k).start()

    def w_copy(k):
        to = plus(t, k, n_t)
        return remote(w_hbm.at[rows_of(to)], w_all.at[t, rows_of(to)], w_ss.at[k], w_rs.at[k],
                      {"tensor": to})

    def w_arrived():
        for k in range(1, n_t):
            place = w_all.at[minus(t, k, n_t), rows_of(t)]
            remote(place, place, w_ss.at[k], w_rs.at[k], {"tensor": plus(t, k, n_t)}).wait_recv()

    for k in range(1, n_t):
        w_copy(k).start()

    for copy in locals_in:
        copy.wait()

    def landed(buffer, send, recv, k):
        source = buffer.at[minus(s, k, n_seq)]
        return remote(source, source, send.at[k], recv.at[k], {"seq": plus(s, k, n_seq)})

    @over_seq
    def _(k):
        landed(keys_all, keys_ss, keys_rs, k).wait_recv()

    vp_acc[...] = jnp.zeros_like(vp_acc)

    @pl.loop(0, heads, unroll=heads)
    def _(h):
        cols = pl.ds(pl.multiple_of(h * HD, HD), HD)
        keys = keys_all[...].reshape(image_total, HD)
        raw = dot(keys, q_ref[0, :, cols], 1, 1) * inv_root
        expo = jnp.exp(raw - raw.max(0, keepdims=True))
        p = expo * (1.0 / expo.sum(0, keepdims=True))
        probs[h] = p
        vp_acc[...] += dot(p.astype(BF16), og_ref[0, :, cols], 1, 0)

    vp_send[...] = vp_acc[...].astype(BF16).reshape(n_seq, img_dev, HD)

    def scatter_copy(src, dst, send, recv, k):
        to = plus(s, k, n_seq)
        return remote(src.at[to], dst.at[s], send.at[k], recv.at[k], {"seq": to})

    @over_seq
    def _(k):
        scatter_copy(vp_send, vp_recv, vp_ss, vp_rs, k).start()

    vp_recv[s] = vp_send[s]

    @over_seq
    def _(k):
        landed(scol, st_ss, st_rs, k).wait_recv()

    if parts > 1:
        w_arrived()

    def weight_part(n):
        return jnp.concatenate([w_all[plus(t, kt, n_t), rows_of(t)] for kt in range(n)], axis=1)

    states = scol[...].reshape(image_total, width)
    sums = dot(states, weight_part(parts), 1, 0)
    for kt in range(parts):
        xp_send[kt] = (
            sums[:, kt * HD : (kt + 1) * HD].reshape(n_seq, img_dev, HD).astype(xp_send.dtype)
        )

    def xp_copy(kt, k):
        to = plus(s, k, n_seq)
        return remote(xp_send.at[kt, to], xp_recv.at[part, s], xp_ss.at[kt, k], xp_rs.at[kt, k],
                      {"seq": to, "tensor": plus(t, kt, n_t)})

    def xp_arrived(kt, k):
        place = xp_recv.at[minus(t, kt, n_t) % parts, minus(s, k, n_seq)]
        return remote(place, place, xp_ss.at[kt, k], xp_rs.at[kt, k],
                      {"seq": plus(s, k, n_seq), "tensor": plus(t, kt, n_t)})

    for kt in range(parts):
        @pl.loop(0 if kt else 1, n_seq)
        def _(k):
            xp_copy(kt, k).start()

    xp_recv[part, s] = xp_send[0, s]

    @over_seq
    def _(k):
        landed(vp_recv, vp_ss, vp_rs, k).wait_recv()

    vg_all[t, s] = vp_recv[...].astype(F32).sum(0).astype(BF16)

    def vg_copy(m):
        return remote(
            vg_all.at[t, s], vg_all.at[t, s], vg_ss.at[m], vg_rs.at[m],
            {"seq": plus(s, m // n_t, n_seq), "tensor": plus(t, m % n_t, n_t)},
        )

    def vg_goes(m):
        if parts > 1:
            return m > 0
        return jnp.logical_or(m % n_t == 0, lax.rem(s, n_t) == plus(t, m % n_t, n_t))

    @pl.loop(1, n_seq * n_t)
    def _(m):
        @pl.when(vg_goes(m))
        def _():
            vg_copy(m).start()

    for kt in range(parts):
        @pl.loop(0 if kt else 1, n_seq)
        def _(k):
            xp_arrived(kt, k).wait_recv()

    val_all[s] = xp_recv[...].astype(F32).sum((0, 1)).astype(BF16)

    def val_copy(k):
        return remote(val_all.at[s], val_all.at[s], val_ss.at[k], val_rs.at[k],
                      {"seq": plus(s, k, n_seq)})

    @over_seq
    def _(k):
        val_copy(k).start()

    @pl.loop(1, n_seq * n_t)
    def _(m):
        from_s = minus(s, m // n_t, n_seq)

        @pl.when(m > 0 if parts > 1 else jnp.logical_or(m % n_t == 0, lax.rem(from_s, n_t) == t))
        def _():
            source = vg_all.at[minus(t, m % n_t, n_t), from_s]
            remote(source, source, vg_ss.at[m], vg_rs.at[m],
                   {"seq": plus(s, m // n_t, n_seq), "tensor": plus(t, m % n_t, n_t)}).wait_recv()

    def grads_of(n):
        return jnp.concatenate(
            [vg_all[plus(t, kt, n_t)].reshape(image_total, HD) for kt in range(n)], axis=1
        )

    terms = dot(scol[...].reshape(image_total, width), grads_of(parts), 0, 0)
    for kt in range(parts):
        wg_send[kt] = terms[:, kt * HD : (kt + 1) * HD].astype(BF16)

    def wg_copy(kd, kt):
        return remote(wg_send.at[kt], wg_recv.at[d, rows_of(t)], wg_ss.at[kd, kt],
                      wg_rs.at[kd, kt],
                      {"dp": plus(d, kd, n_dp), "tensor": plus(t, kt, n_t)})

    wg_moves = [(kd, kt) for kd in range(n_dp) for kt in range(parts) if kd + kt > 0]
    for kd, kt in wg_moves:
        wg_copy(kd, kt).start()
    wg_recv[d, rows_of(t)] = wg_send[0]

    if parts == 1:
        w_arrived()

    def image_term(c):
        rows = jnp.concatenate([vg_all[c, j * n_t + t] for j in range(per_t)], axis=0)
        return dot(rows, w_all[c], 1, 1).astype(BF16).astype(F32)

    if parts > 1:
        total = dot(grads_of(n_t), weight_part(n_t), 1, 1)
    else:
        total = image_term(0)
        for c in range(1, n_t):
            total = total + image_term(c)
    blocks = ig_send.shape[0]
    ig_send[...] = total.astype(BF16).reshape(blocks, img_dev, width)

    to_t = s // per_t
    slot = cols_of(lax.rem(s, per_t))
    place_in = lax.rem(s, per_t) * parts + part

    def row_block(j):
        return j if parts > 1 else j * n_t + t

    def ig_copy(j):
        return remote(ig_send.at[j], ig_recv.at[:, slot], ig_ss.at[j], ig_rs.at[place_in],
                      {"seq": row_block(j), "tensor": to_t})

    def ig_stays(j):
        return jnp.logical_and(row_block(j) == s, to_t == t)

    for j in range(blocks):
        @pl.when(jnp.logical_not(ig_stays(j)))
        def _():
            ig_copy(j).start()

        @pl.when(ig_stays(j))
        def _():
            ig_recv[:, slot] = ig_send[j]

    @over_seq
    def _(k):
        landed(val_all, val_ss, val_rs, k).wait_recv()

    kp_acc[...] = jnp.zeros_like(kp_acc)

    @pl.loop(0, heads, unroll=heads)
    def _(h):
        cols = pl.ds(pl.multiple_of(h * HD, HD), HD)
        slopes = dot(val_all[...].reshape(image_total, HD), og_ref[0, :, cols], 1, 1)
        p = probs[h]
        delta = (p * slopes).sum(0, keepdims=True)
        ds = (p * (slopes - delta) * inv_root).astype(BF16)
        kp_acc[...] += dot(ds, q_ref[0, :, cols], 1, 0)
        keys = keys_all[...].reshape(image_total, HD)
        qg_ref[0, :, cols] = dot(ds, keys, 0, 0).astype(BF16)

    qg_out = pltpu.make_async_copy(qg_ref, qg_hbm, out_sem.at[0])
    qg_out.start()
    kp_send[...] = kp_acc[...].astype(BF16).reshape(n_seq, img_dev, HD)

    @over_seq
    def _(k):
        scatter_copy(kp_send, kp_recv, kp_ss, kp_rs, k).start()

    kp_recv[s] = kp_send[s]

    for kd, kt in wg_moves:
        place = wg_recv.at[minus(d, kd, n_dp), rows_of(minus(t, kt, n_t))]
        remote(place, place, wg_ss.at[kd, kt], wg_rs.at[kd, kt],
               {"dp": plus(d, kd, n_dp), "tensor": plus(t, kt, n_t)}).wait_recv()
    wg_ref[...] = wg_recv[...].astype(F32).sum(0).astype(BF16)
    wg_out = pltpu.make_async_copy(wg_ref, wg_hbm, out_sem.at[1])
    wg_out.start()

    for j in range(per_t * parts):
        from_s = t * per_t + j // parts
        from_t = j % parts if parts > 1 else lax.rem(s, n_t)

        @pl.when(jnp.logical_not(jnp.logical_and(from_s == s, from_t == t)))
        def _():
            place = ig_recv.at[:, pl.ds(j * width, width)]
            remote(ig_send.at[0], place, ig_ss.at[j], ig_rs.at[j],
                   {"seq": from_s, "tensor": from_t}).wait_recv()

    ig_out = pltpu.make_async_copy(ig_recv, ig_hbm.at[0], out_sem.at[2])
    ig_out.start()

    @over_seq
    def _(k):
        landed(kp_recv, kp_ss, kp_rs, k).wait_recv()

    kg_ref[0] = kp_recv[...].astype(F32).sum(0).astype(BF16)

    kg_out = pltpu.make_async_copy(kg_ref, kg_hbm, out_sem.at[3])
    kg_out.start()

    for kt in range(parts):
        @pl.loop(0 if kt else 1, n_seq)
        def _(k):
            xp_copy(kt, k).wait_send()

    @over_seq
    def _(k):
        keys_copy(k).wait_send()
        st_copy(k).wait_send()
        scatter_copy(vp_send, vp_recv, vp_ss, vp_rs, k).wait_send()
        val_copy(k).wait_send()
        scatter_copy(kp_send, kp_recv, kp_ss, kp_rs, k).wait_send()

    @pl.loop(1, n_seq * n_t)
    def _(m):
        @pl.when(vg_goes(m))
        def _():
            vg_copy(m).wait_send()

    for k in range(1, n_t):
        w_copy(k).wait_send()
    for kd, kt in wg_moves:
        wg_copy(kd, kt).wait_send()
    for j in range(blocks):
        @pl.when(jnp.logical_not(ig_stays(j)))
        def _():
            ig_copy(j).wait_send()
    for copy in (qg_out, wg_out, ig_out, kg_out):
        copy.wait()


def write_out(*refs):
    copies = [pltpu.make_async_copy(refs[i], refs[4 + i], refs[8].at[i]) for i in range(4)]
    for copy in copies:
        copy.start()
    for copy in copies:
        copy.wait()


def on_device(n_dp, n_seq, n_t, queries, image_keys, image_states, value_weight, out_grad):
    img_dev = image_keys.shape[1]
    image_total = n_seq * img_dev
    text_rows = queries.shape[1]
    heads = queries.shape[2] // HD
    d_model = image_states.shape[2]
    d_seq = value_weight.shape[0]
    d_t = d_model // n_t
    per_t = n_seq // n_t
    parts = n_t if d_seq % (n_t * 128) == 0 else 1
    width = d_seq // parts
    vmem = pltpu.VMEM
    rows = (n_seq, img_dev, HD)
    scratch = [
        vmem(queries.shape, BF16),
        vmem(image_keys.shape, BF16),
        vmem(value_weight.shape, BF16),
        vmem((1, img_dev, d_t), BF16),
        vmem(queries.shape, BF16),
        vmem(out_grad.shape, BF16),
        vmem(rows, BF16),
        vmem((n_seq, img_dev, width), BF16),
        vmem((n_t, d_seq, HD), BF16),
        vmem((heads, image_total, text_rows), F32),
        vmem((image_total, HD), F32),
        vmem(rows, BF16),
        vmem(rows, BF16),
        vmem((parts,) + rows, XP),
        vmem((parts,) + rows, XP),
        vmem((n_t,) + rows, BF16),
        vmem(rows, BF16),
        vmem((image_total, HD), F32),
        vmem(rows, BF16),
        vmem(rows, BF16),
        vmem((parts, width, HD), BF16),
        vmem((n_dp, d_seq, HD), BF16),
        vmem((per_t * parts, img_dev, width), BF16),
        vmem((img_dev, d_t), BF16),
    ]
    counts = [
        (n_seq,), (n_seq,), (n_t,), (n_seq,), (parts, n_seq), (n_seq * n_t,), (n_seq,), (n_seq,),
        (n_dp, parts), (per_t * parts,),
    ]
    sems = [pltpu.SemaphoreType.DMA((4,))] + [pltpu.SemaphoreType.DMA((5,))] + [pltpu.SemaphoreType.DMA(c) for c in counts for _ in range(2)]
    spec = pl.BlockSpec(memory_space=pltpu.VMEM)
    grads = pl.pallas_call(
        functools.partial(kernel, n_dp, n_seq, n_t),
        out_shape=(
            jax.ShapeDtypeStruct(queries.shape, BF16),
            jax.ShapeDtypeStruct(image_keys.shape, BF16),
            jax.ShapeDtypeStruct(value_weight.shape, BF16),
            jax.ShapeDtypeStruct((1, img_dev, d_t), BF16),
        ),
        in_specs=[pl.BlockSpec(memory_space=pltpu.HBM)] * 5,
        out_specs=(pl.BlockSpec(memory_space=pltpu.HBM),) * 4,
        scratch_shapes=scratch + sems,
        compiler_params=pltpu.CompilerParams(
            collective_id=0, has_side_effects=True, vmem_limit_bytes=63 * 1024 * 1024
        ),
    )(queries, image_keys, image_states, value_weight, out_grad)
    return pl.pallas_call(
        write_out,
        out_shape=tuple(jax.ShapeDtypeStruct(g.shape, g.dtype) for g in grads),
        in_specs=[spec] * 4,
        out_specs=(pl.BlockSpec(memory_space=pltpu.HBM),) * 4,
        scratch_shapes=[pltpu.SemaphoreType.DMA((4,))],
    )(*grads)


def solution(mesh):
    in_specs = (
        P("dp", "seq", "tensor"),
        P("dp", "seq", "tensor"),
        P("dp", "seq", None),
        P("seq", "tensor"),
        P("dp", "seq", "tensor"),
    )
    out_specs = (
        P("dp", "seq", "tensor"),
        P("dp", "seq", "tensor"),
        P("seq", "tensor"),
        P("dp", "seq", "tensor"),
    )
    sizes = (mesh.shape["dp"], mesh.shape["seq"], mesh.shape["tensor"])
    return jax.shard_map(
        functools.partial(on_device, *sizes),
        mesh=mesh, in_specs=in_specs, out_specs=out_specs, check_vma=False,
    )
```

time: 55.4 us -> 38.3 us (0.69)
  Pallas kernels: 46.9 us -> 37.5 us
  local copies, waits for them, and re-layouts: 7.56 us -> 0 us
    pallas_call x1, Pallas kernels: 46.9 us -> 35.3 us  [on_device(): pl.pallas_call(functools.partial(kernel, n_dp, n_seq, n_t), out_shape=(ja...]
    unnamed x14 -> x0, local copies, waits for them, and re-layouts: 7.56 us -> none
    pallas_call x0 -> x1, Pallas kernels: none -> 2.2 us  [on_device(): pl.pallas_call(write_out, out_shape=tuple((jax.ShapeDtypeStruct(g.shape,...]
where the time goes in v2:
time: 38.3 us; the launch traced here: 38.1 us
  Pallas kernels  37.5 us (98%)
  between operations  0.64 us (2%)
    pallas_call x1, Pallas kernels, on_device(): pl.pallas_call(functools.partial(kernel, n_dp, n_seq, n_t), out_shape=(ja...  35.3 us
    pallas_call x1, Pallas kernels, on_device(): pl.pallas_call(write_out, out_shape=tuple((jax.ShapeDtypeStruct(g.shape,...  2.2 us

profile of v2, /device:TPU:0, one launch (start us, length us, event | category | flops | bytes accessed | tf_op | source)
XLA Modules:
  0.0 38.1 jit_solution(9237642369794106614)
XLA Ops:
  0.6 35.3 %shard_map.84 = (bf16[1,256,1024]{2,1,0:T(8,128)(2,1)}, bf16[1,32,128]{2,1,0:T(8,128)(2,1)}, bf16[1024,128]{1,0:T(8,128)(2,1)}, bf16[1,32,4096]{2,1,0:T(8,128)(2,1)}) custom-call(bf16[1,256,1024]{2,1,0:T(8,128)(2,1)} %q_hbm.1, bf16[1,32,128]{2,1,0:T(8,128)(2,1)} %k_hbm.1, bf16[1,32,8192]{2,1,0:T(8,128)(2,1)} %st_hbm.1, bf16[1024,128]{1,0:T(8,128)(2,1)} %w_hbm.1, ...), custom_call_target="tpu_custom_call" | custom-call | tf_op jit(solution)/shard_map/pallas_call | solution.py:439
  35.9 2.2 %shard_map.85 = (bf16[1,256,1024]{2,1,0:T(8,128)(2,1)}, bf16[1,32,128]{2,1,0:T(8,128)(2,1)}, bf16[1024,128]{1,0:T(8,128)(2,1)}, bf16[1,32,4096]{2,1,0:T(8,128)(2,1)}) custom-call(bf16[1,256,1024]{2,1,0:T(8,128)(2,1)} %get-tuple-element.8.refs_0_, bf16[1,32,128]{2,1,0:T(8,128)(2,1)} %get-tuple-element.9.refs_1_, bf16[1024,128]{1,0:T(8,128)(2,1)} %get-tuple-element.10.refs_2_, ...), custom_call_target="tpu_custom_call" | custom-call | tf_op jit(solution)/shard_map/pallas_call | solution.py:454

commit v3 on v2

--- a/solution.py
+++ b/solution.py
@@ -23,7 +23,7 @@
     n_dp, n_seq, n_t,
     q_hbm, k_hbm, st_hbm, w_hbm, og_hbm,
     qg_hbm, kg_hbm, wg_hbm, ig_hbm,
-    qg_ref, kg_ref, wg_ref, ig_ref, q_ref, og_ref, keys_all, scol, w_all, probs, vp_acc, vp_send, vp_recv, xp_send, xp_recv,
+    qg_ref, kg_ref, wg_ref, ig_ref, q_ref, og_ref, keys_all, scol, turned, w_all, probs, vp_acc, vp_send, vp_recv, xp_send, xp_recv,
     vg_all, val_all, kp_acc, kp_send, kp_recv, wg_send, wg_recv, ig_send, ig_recv,
     out_sem, in_sem, keys_ss, keys_rs, st_ss, st_rs, w_ss, w_rs, vp_ss, vp_rs, xp_ss, xp_rs,
     vg_ss, vg_rs, val_ss, val_rs, kp_ss, kp_rs, wg_ss, wg_rs, ig_ss, ig_rs,
@@ -188,6 +188,7 @@
             xp_copy(kt, k).start()
 
     xp_recv[part, s] = xp_send[0, s]
+    turned[...] = scol[...].reshape(image_total, width).T
 
     @over_seq
     def _(k):
@@ -242,7 +243,7 @@
             [vg_all[plus(t, kt, n_t)].reshape(image_total, HD) for kt in range(n)], axis=1
         )
 
-    terms = dot(scol[...].reshape(image_total, width), grads_of(parts), 0, 0)
+    terms = dot(turned[...], grads_of(parts), 1, 0)
     for kt in range(parts):
         wg_send[kt] = terms[:, kt * HD : (kt + 1) * HD].astype(BF16)
 
@@ -251,7 +252,7 @@
                       wg_rs.at[kd, kt],
                       {"dp": plus(d, kd, n_dp), "tensor": plus(t, kt, n_t)})
 
-    wg_moves = [(kd, kt) for kd in range(n_dp) for kt in range(parts) if kd + kt > 0]
+    wg_moves = [(kd, kt) for kd in reversed(range(n_dp)) for kt in range(parts) if kd + kt > 0]
     for kd, kt in wg_moves:
         wg_copy(kd, kt).start()
     wg_recv[d, rows_of(t)] = wg_send[0]
@@ -384,10 +385,15 @@
 
 
 def write_out(*refs):
-    copies = [pltpu.make_async_copy(refs[i], refs[4 + i], refs[8].at[i]) for i in range(4)]
-    for copy in copies:
+    sems = refs[12]
+    ins = [pltpu.make_async_copy(refs[i], refs[8 + i], sems.at[0, i]) for i in range(4)]
+    outs = [pltpu.make_async_copy(refs[8 + i], refs[4 + i], sems.at[1, i]) for i in range(4)]
+    for copy in ins:
         copy.start()
-    for copy in copies:
+    for arrived, leaves in zip(ins, outs):
+        arrived.wait()
+        leaves.start()
+    for copy in outs:
         copy.wait()
 
 
@@ -413,6 +419,7 @@
         vmem(out_grad.shape, BF16),
         vmem(rows, BF16),
         vmem((n_seq, img_dev, width), BF16),
+        vmem((width, image_total), BF16),
         vmem((n_t, d_seq, HD), BF16),
         vmem((heads, image_total, text_rows), F32),
         vmem((image_total, HD), F32),
@@ -454,9 +461,10 @@
     return pl.pallas_call(
         write_out,
         out_shape=tuple(jax.ShapeDtypeStruct(g.shape, g.dtype) for g in grads),
-        in_specs=[spec] * 4,
+        in_specs=[pl.BlockSpec(memory_space=pltpu.HBM)] * 4,
         out_specs=(pl.BlockSpec(memory_space=pltpu.HBM),) * 4,
-        scratch_shapes=[pltpu.SemaphoreType.DMA((4,))],
+        scratch_shapes=[vmem(g.shape, g.dtype) for g in grads] + [pltpu.SemaphoreType.DMA((2, 4))],
+        compiler_params=pltpu.CompilerParams(vmem_limit_bytes=63 * 1024 * 1024),
     )(*grads)
 
 

time: 38.3 us -> 38.1 us (level)
  no operation moved by 1% of the time
where the time goes in v3:
time: 38.1 us; the launch traced here: 38 us
  Pallas kernels  37.4 us (98%)
  between operations  0.64 us (2%)
    pallas_call x1, Pallas kernels, on_device(): pl.pallas_call(functools.partial(kernel, n_dp, n_seq, n_t), out_shape=(ja...  35.3 us
    pallas_call x1, Pallas kernels, on_device(): pl.pallas_call(write_out, out_shape=tuple((jax.ShapeDtypeStruct(g.shape,...  2.08 us

profile of v3, /device:TPU:0, one launch (start us, length us, event | category | flops | bytes accessed | tf_op | source)
XLA Modules:
  0.0 38.0 jit_solution(8613668711883479200)
XLA Ops:
  0.6 35.3 %shard_map.84 = (bf16[1,256,1024]{2,1,0:T(8,128)(2,1)}, bf16[1,32,128]{2,1,0:T(8,128)(2,1)}, bf16[1024,128]{1,0:T(8,128)(2,1)}, bf16[1,32,4096]{2,1,0:T(8,128)(2,1)}) custom-call(bf16[1,256,1024]{2,1,0:T(8,128)(2,1)} %q_hbm.1, bf16[1,32,128]{2,1,0:T(8,128)(2,1)} %k_hbm.1, bf16[1,32,8192]{2,1,0:T(8,128)(2,1)} %st_hbm.1, bf16[1024,128]{1,0:T(8,128)(2,1)} %w_hbm.1, ...), custom_call_target="tpu_custom_call" | custom-call | tf_op jit(solution)/shard_map/pallas_call | solution.py:446
  35.9 2.1 %shard_map.85 = (bf16[1,256,1024]{2,1,0:T(8,128)(2,1)}, bf16[1,32,128]{2,1,0:T(8,128)(2,1)}, bf16[1024,128]{1,0:T(8,128)(2,1)}, bf16[1,32,4096]{2,1,0:T(8,128)(2,1)}) custom-call(bf16[1,256,1024]{2,1,0:T(8,128)(2,1)} %get-tuple-element.8.refs_0_, bf16[1,32,128]{2,1,0:T(8,128)(2,1)} %get-tuple-element.9.refs_1_, bf16[1024,128]{1,0:T(8,128)(2,1)} %get-tuple-element.10.refs_2_, ...), custom_call_target="tpu_custom_call" | custom-call | tf_op jit(solution)/shard_map/pallas_call | solution.py:461
